TPU v7x, 32 devices: a whole 2x2x4 slice. The times are simulated.
32 devices in a mesh: groups: 2 (over y), seq: 4 (over z), mp: 4 (over x, core).
Axes of the slice: x: 2, y: 2, z: 4, core: 2. Of those that a mesh axis runs over, the one named last changes fastest.
Arguments:
- hidden_prompt: bfloat16 [2048, 5120], P(('groups', 'seq'), 'mp'), parts along dimension 0, may hold values from -40 to 40
- hidden_comp: bfloat16 [1024, 5120], P(('groups', 'seq'), 'mp'), parts along dimension 0, may hold values from -40 to 40
- w_query: bfloat16 [5120, 5120], P(None, 'mp'), may hold values from -0.078125 to 0.078125
- w_key: bfloat16 [5120, 1024], P(None, 'mp'), may hold values from -0.078125 to 0.078125
- w_value: bfloat16 [5120, 1024], P(None, 'mp'), may hold values from -0.078125 to 0.078125
- lengths: int32 [32], P('groups'), parts along dimension 0, may hold values from 1 to 256, 512 in all
- row_owner: int32 [1024, 1], P(('groups', 'seq')), parts along dimension 0, may hold values from 0 to 3; in each aligned block of 128 rows (0 to 127, 128 to 255, ...) at most 64 rows name the same one
Outputs:
- prompt_out: bfloat16 [2048, 5120], P(('groups', 'seq'), 'mp'), parts along dimension 0
- comp_out: bfloat16 [2048, 5120], P(('groups', 'seq'), 'mp'), parts along dimension 0
There are 2 independent parts, one for each index of `groups`. A program takes and returns all parts, laid end to end along the dimension named above; an argument that names none is the same for every part. Nothing has to cross between parts.
Inputs may be any that keep to these rules, and one draw needn't show every extreme that they name: The lengths sum to 512, and the largest is exactly 256. `row_owner`: in every aligned block of 128 rows no owner is named more than 64 times, and in some blocks one owner is named exactly 64 times.
All inputs are finite; a program needn't handle non-finite values.
Results may differ from a plain program's by a relative error of at most 0.0072.
Values may be sent and summed in bfloat16 or wider, within the bound.
A program may use at most 128 MiB of HBM per device.

v0:
```python
import jax
import jax.numpy as jnp
from jax import lax
from jax.sharding import PartitionSpec as P

HD = 128


rope_base = 1000000.0


def rotate(matrix_in, positions):
    row_count = matrix_in.shape[0]
    head_count = matrix_in.shape[1] // HD
    half_size = HD // 2
    inverse_freq = rope_base ** (-2.0 * jnp.arange(half_size, dtype=jnp.float32) / HD)
    angles = positions.astype(jnp.float32)[:, None] * inverse_freq[None, :]
    cosine = jnp.cos(angles)[:, None, :]
    sine_part = jnp.sin(angles)[:, None, :]
    shaped = matrix_in.reshape(row_count, head_count, HD)
    front_half = shaped[..., :half_size]
    back_half = shaped[..., half_size:]
    rotated = jnp.concatenate(
        [front_half * cosine - back_half * sine_part, back_half * cosine + front_half * sine_part],
        -1,
    )
    return rotated.reshape(row_count, head_count * HD)


def project(hidden, weight, positions, with_rope):
    product = jnp.dot(hidden, weight, preferred_element_type=jnp.float32)
    if with_rope:
        product = rotate(product, positions)
    return product.astype(jnp.bfloat16)


def attend(queries, key_rows, value_rows, allowed):
    row_count = queries.shape[0]
    head_count = queries.shape[1] // HD
    kv_count = key_rows.shape[1] // HD
    group_size = head_count // kv_count
    query_heads = queries.reshape(row_count, head_count, HD).transpose(1, 0, 2)
    key_heads = key_rows.reshape(-1, kv_count, HD).transpose(1, 0, 2)
    value_heads = value_rows.reshape(-1, kv_count, HD).transpose(1, 0, 2)

    def single_head(inputs_one):
        query_head, head_index = inputs_one
        key_head = lax.dynamic_index_in_dim(key_heads, head_index // group_size, 0, keepdims=False)
        value_head = lax.dynamic_index_in_dim(
            value_heads, head_index // group_size, 0, keepdims=False
        )
        scores = jnp.dot(query_head, key_head.T, preferred_element_type=jnp.float32) * HD ** (-0.5)
        scores = jnp.where(allowed, scores, -jnp.inf)
        row_max = jnp.max(scores, 1, keepdims=True)
        weights = jnp.exp(scores - row_max)
        row_total = jnp.sum(weights, 1, keepdims=True)
        mixed = jnp.dot(
            weights.astype(jnp.bfloat16), value_head, preferred_element_type=jnp.float32
        )
        return (mixed / row_total).astype(jnp.bfloat16)

    outputs = lax.map(single_head, (query_heads, jnp.arange(head_count, dtype=jnp.int32)))
    return outputs.transpose(1, 0, 2).reshape(row_count, head_count * HD)


def completion_starts(lengths, row_index):
    comp_ends = jnp.cumsum(lengths)
    preceding = comp_ends[None, :] <= row_index[:, None]
    return jnp.sum(jnp.where(preceding, lengths[None, :], 0), 1)


def owner_rank(owners, owner_count):
    chosen = (owners[:, None] == jnp.arange(owner_count, dtype=jnp.int32)[None, :]).astype(
        jnp.int32
    )
    earlier = jnp.cumsum(chosen, 0) - chosen
    return jnp.sum(earlier * chosen, 1)


def local(hidden_prompt, hidden_comp, w_query, w_key, w_value, lengths, row_owner):
    full_prompt, full_comp = (
        lax.all_gather(hidden_prompt, "mp", axis=1, tiled=True),
        lax.all_gather(hidden_comp, "mp", axis=1, tiled=True),
    )
    prompt_rows = hidden_prompt.shape[0]
    comp_rows = hidden_comp.shape[0]
    seq_count = lax.axis_size("seq")
    seq_index = lax.axis_index("seq")
    capacity = 2 * comp_rows // seq_count
    prompt_pos = seq_index * prompt_rows + jnp.arange(prompt_rows, dtype=jnp.int32)
    comp_index = seq_index * comp_rows + jnp.arange(comp_rows, dtype=jnp.int32)
    starts = completion_starts(lengths, comp_index)
    comp_pos = seq_count * prompt_rows + comp_index - starts
    query_prompt = project(full_prompt, w_query, prompt_pos, True)
    key_prompt = project(full_prompt, w_key, prompt_pos, True)
    value_prompt = project(full_prompt, w_value, prompt_pos, False)
    query_comp = project(full_comp, w_query, comp_pos, True)
    key_comp = project(full_comp, w_key, comp_pos, True)
    value_comp = project(full_comp, w_value, comp_pos, False)
    prompt_keys, prompt_values = (
        lax.all_gather(key_prompt, "seq", axis=0, tiled=True),
        lax.all_gather(value_prompt, "seq", axis=0, tiled=True),
    )
    total_prompt = prompt_keys.shape[0]
    key_positions = jnp.arange(total_prompt, dtype=jnp.int32)
    prompt_out = attend(
        query_prompt, prompt_keys, prompt_values, key_positions[None, :] <= prompt_pos[:, None]
    )
    owners = row_owner[:, 0]
    slot_index = owners * capacity + owner_rank(owners, seq_count)
    query_width = query_comp.shape[1]
    outgoing = (
        jnp.zeros((seq_count * capacity, query_width), jnp.bfloat16).at[slot_index].set(query_comp)
    )
    rows_sent = jnp.full((seq_count * capacity,), -1, jnp.int32).at[slot_index].set(comp_index)
    arrived, arrived_rows = (
        lax.all_to_all(outgoing, "seq", split_axis=0, concat_axis=0, tiled=True),
        lax.all_to_all(rows_sent, "seq", split_axis=0, concat_axis=0, tiled=True),
    )
    comp_keys, comp_values = (
        lax.all_gather(key_comp, "seq", axis=0, tiled=True),
        lax.all_gather(value_comp, "seq", axis=0, tiled=True),
    )
    comp_all = jnp.arange(comp_keys.shape[0], dtype=jnp.int32)
    arrived_starts = completion_starts(lengths, arrived_rows)
    own_keys = (comp_all[None, :] >= arrived_starts[:, None]) & (
        comp_all[None, :] <= arrived_rows[:, None]
    )
    allowed = jnp.concatenate([jnp.ones((arrived.shape[0], total_prompt), bool), own_keys], 1)
    key_rows = jnp.concatenate([prompt_keys, comp_keys], 0)
    value_rows = jnp.concatenate([prompt_values, comp_values], 0)
    attended = attend(arrived, key_rows, value_rows, allowed)
    comp_out = jnp.where(arrived_rows[:, None] >= 0, attended, jnp.zeros_like(attended))
    return (prompt_out, comp_out)


def solution(mesh):
    placed = (
        P(("groups", "seq"), "mp"),
        P(("groups", "seq"), "mp"),
        P(None, "mp"),
        P(None, "mp"),
        P(None, "mp"),
        P("groups"),
        P(("groups", "seq"), None),
    )
    return jax.shard_map(
        local,
        mesh=mesh,
        in_specs=placed,
        out_specs=(P(("groups", "seq"), "mp"), P(("groups", "seq"), "mp")),
        check_vma=False,
    )
```

profile of v0, /device:TPU:0, one launch (start us, length us, event | category | flops | bytes accessed | tf_op | source)
XLA Modules:
  0.0 266.2 jit_solution(18395778464242747017)
XLA Ops:
  12.0 6.3 %all-to-all-start = ((s32[4,64,1]{1,2,0:T(1,128)}), s32[4,64,1]{1,2,0:T(1,128)S(1)}, u32[]{:S(2)}, u32[]{:S(2)}) async-start(s32[4,64,1]{1,2,0:T(1,128)} %bitcast.18), calls=%async_computation | async-start | bytes 4096 | tf_op jit(solution)/shard_map/all_to_all | solution.py:118
  22.1 1.7 all-to-all-done
  25.6 4.9 %all-gather.5.cloned.1.call-done = bf16[128,5120]{1,0:T(8,128)(2,1)} async-done(((bf16[128,1280]{1,0:T(8,128)(2,1)}), bf16[128,5120]{1,0:T(8,128)(2,1)}) %all-gather.5.cloned.1.call-update) | async-done | bytes 1310736 | tf_op jit(solution)/shard_map/all_gather | solution.py:83
  30.5 8.6 %fusion.44 = f32[128,1280]{0,1:T(8,128)S(1)} fusion(bf16[128,5120]{1,0:T(8,128)(2,1)} %all-gather.5.cloned.1.call-done, bf16[5120,1280]{1,0:T(8,128)(2,1)} %param.13), kind=kOutput, calls=%fused_computation.88 | convolution fusion | flops 1677721600 | bytes 15073280 | tf_op jit(solution)/shard_map/dot_general | solution.py:31
  40.1 2.5 scatter_custom_fusion.1
  42.6 4.6 %all-to-all-start.1 = ((bf16[4,64,1280]{2,1,0:T(8,128)(2,1)}), bf16[4,64,1280]{2,1,0:T(8,128)(2,1)}, u32[]{:S(2)}, u32[]{:S(2)}) async-start(bf16[4,64,1280]{2,1,0:T(8,128)(2,1)} %bitcast.122), calls=%async_computation.1 | async-start | bytes 1310720 | tf_op jit(solution)/shard_map/all_to_all | solution.py:117
  47.2 1.9 fusion.45
  49.8 22.7 %all_gather.22 = bf16[512,256]{0,1:T(8,128)(2,1)} all-gather(bf16[128,256]{0,1:T(8,128)(2,1)S(1)} %bitcast.129), channel_id=1, replica_groups=mesh['groups'=2,'seq'=4,'mp'=4] {'seq'}, dimensions={0}, use_global_device_ids=true | all-gather | bytes 327680 | tf_op jit(solution)/shard_map/all_gather | solution.py:121
  72.5 2.7 convolution_convert_fusion.1
  75.2 15.1 %all_gather.23 = bf16[512,256]{1,0:T(8,128)(2,1)} all-gather(bf16[128,256]{1,0:T(8,128)(2,1)S(1)} %convolution_convert_fusion.1), channel_id=1, replica_groups=mesh['groups'=2,'seq'=4,'mp'=4] {'seq'}, dimensions={0}, use_global_device_ids=true | all-gather | bytes 327680 | tf_op jit(solution)/shard_map/all_gather | solution.py:122
  90.2 2.3 reshape.234
  92.5 2.2 copy.67
  94.7 10.7 %fusion.42 = f32[256,1280]{0,1:T(8,128)S(1)} fusion(bf16[256,5120]{1,0:T(8,128)(2,1)} %all-gather.3.cloned.1.call-done, bf16[5120,1280]{1,0:T(8,128)(2,1)} %param.13), kind=kOutput, calls=%fused_computation.86 | convolution fusion | flops 3355443200 | bytes 17039360 | tf_op jit(solution)/shard_map/dot_general | solution.py:31
  107.0 16.2 %all_gather.19 = bf16[1024,256]{0,1:T(8,128)(2,1)} all-gather(bf16[256,256]{0,1:T(8,128)(2,1)S(1)} %bitcast.128), channel_id=1, replica_groups=mesh['groups'=2,'seq'=4,'mp'=4] {'seq'}, dimensions={0}, use_global_device_ids=true | all-gather | bytes 655360 | tf_op jit(solution)/shard_map/all_gather | solution.py:101
  124.1 14.8 %all_gather.20 = bf16[1024,256]{1,0:T(8,128)(2,1)S(1)} all-gather(bf16[256,256]{1,0:T(8,128)(2,1)S(1)} %convolution_convert_fusion), channel_id=1, replica_groups=mesh['groups'=2,'seq'=4,'mp'=4] {'seq'}, dimensions={0}, use_global_device_ids=true | all-gather | bytes 655360 | tf_op jit(solution)/shard_map/all_gather | solution.py:102
  142.3 52.2 %while.26 = (s32[]{:T(128)}, bf16[10,256,128]{1,2,0:T(8,128)(2,1)}, bf16[10,256,128]{1,2,0:T(8,128)(2,1)}, s32[10]{0:T(128)S(1)}, bf16[2,1024,128]{1,2,0:T(8,128...) while((s32[]{:T(128)}, bf16[10,256,128]{1,2,0:T(8,128)(2,1)}, ...), condition=%wide.region_3.4_spmd.clone, body=%wide.region_0.3_spmd.clone.sunk | while | flops 136379920 | bytes 6166837 | solution.py:62
  144.6 1.5 fusion.76
  149.9 1.5 fusion.76
  155.1 1.5 fusion.76
  194.5 2.2 copy.71
  196.8 2.1 pad_maximum_fusion
  200.7 56.3 %while.25 = (s32[]{:T(128)}, bf16[10,256,128]{1,2,0:T(8,128)(2,1)}, bf16[10,256,128]{2,1,0:T(8,128)(2,1)}, s32[10]{0:T(128)S(1)}, bf16[2,1536,128]{1,2,0:T(8,128...) while((s32[]{:T(128)}, bf16[10,256,128]{1,2,0:T(8,128)(2,1)}, ...), condition=%wide.region_14.15_spmd, body=%wide.region_11.14_spmd.sunk | while | flops 204144144 | bytes 9442613 | solution.py:62
  203.2 1.6 fusion.71
  208.8 1.6 fusion.71
  214.5 1.6 fusion.71
  220.1 1.6 fusion.71
  225.7 1.6 fusion.71
  231.4 1.6 fusion.71
  237.0 1.6 fusion.71
  242.6 1.6 fusion.71
  248.3 1.6 fusion.71
  253.9 1.6 fusion.71
  (217 shorter events, 73.5 us)
Async XLA Ops:
  7.2 40.1 %copy-start = (bf16[5120,256]{1,0:T(8,128)(2,1)S(1)}, bf16[5120,256]{1,0:T(8,128)(2,1)}, u32[]{:S(2)}) copy-start(bf16[5120,256]{1,0:T(8,128)(2,1)} %param.14) | copy-start | bytes 7864324
  7.2 17.9 %copy-start.9 = (s32[16]{0:T(128)S(1)}, s32[16]{0:T(128)}, u32[]{:S(2)}) copy-start(s32[16]{0:T(128)} %param.16) | copy-start | bytes 196
  7.2 23.3 %all-gather.5.cloned.1.call-start = ((), (), s32[]{:S(2)}) async-start(), calls=%async_computation.3 | async-start | bytes 1638400 | tf_op jit(solution)/shard_map/all_gather | solution.py:83
  12.0 11.8 %all-to-all-start = ((s32[4,64,1]{1,2,0:T(1,128)}), s32[4,64,1]{1,2,0:T(1,128)S(1)}, u32[]{:S(2)}, u32[]{:S(2)}) async-start(s32[4,64,1]{1,2,0:T(1,128)} %bitcast.18), calls=%async_computation | async-start | bytes 4096 | tf_op jit(solution)/shard_map/all_to_all | solution.py:118
  18.4 76.4 %all-gather.3.cloned.1.call-start = ((), (), s32[]{:S(2)}) async-start(), calls=%async_computation.2 | async-start | bytes 3276800 | tf_op jit(solution)/shard_map/all_gather | solution.py:82
  42.6 47.6 %all-to-all-start.1 = ((bf16[4,64,1280]{2,1,0:T(8,128)(2,1)}), bf16[4,64,1280]{2,1,0:T(8,128)(2,1)}, u32[]{:S(2)}, u32[]{:S(2)}) async-start(bf16[4,64,1280]{2,1,0:T(8,128)(2,1)} %bitcast.122), calls=%async_computation.1 | async-start | bytes 1310720 | tf_op jit(solution)/shard_map/all_to_all | solution.py:117
  47.2 1.9 copy-start.8
  94.7 11.0 %copy-start.4 = (bf16[256,5120]{1,0:T(8,128)(2,1)S(1)}, bf16[256,5120]{1,0:T(8,128)(2,1)}, u32[]{:S(2)}) copy-start(bf16[256,5120]{1,0:T(8,128)(2,1)} %all-gather.3.cloned.1.call-done) | copy-start | bytes 7864324
  105.7 17.5 %copy-start.5 = (bf16[5120,256]{1,0:T(8,128)(2,1)S(1)}, bf16[5120,256]{1,0:T(8,128)(2,1)}, u32[]{:S(2)}) copy-start(bf16[5120,256]{1,0:T(8,128)(2,1)} %param.15) | copy-start | bytes 7864324
  138.9 0.8 copy-start.2
  144.6 1.8 copy-start.7
  149.8 1.8 copy-start.7
  155.1 1.8 copy-start.7
  160.3 1.8 copy-start.7
  165.5 1.8 copy-start.7
  170.7 1.8 copy-start.7
  176.0 1.8 copy-start.7
  181.2 1.8 copy-start.7
  186.4 1.8 copy-start.7
  191.6 1.8 copy-start.7
  194.5 4.3 %copy-start.3 = (bf16[1024,256]{1,0:T(8,128)(2,1)S(1)}, bf16[1024,256]{1,0:T(8,128)(2,1)}, u32[]{:S(2)}) copy-start(bf16[1024,256]{1,0:T(8,128)(2,1)} %copy-done.2) | copy-start | bytes 1572868
  196.8 2.1 copy-start.6
  203.2 2.0 copy-start.1
  208.8 2.0 copy-start.1
  214.5 2.0 copy-start.1
  220.1 2.0 copy-start.1
  225.7 2.0 copy-start.1
  231.4 2.0 copy-start.1
  237.0 2.0 copy-start.1
  242.6 2.0 copy-start.1
  248.3 2.0 copy-start.1
  253.9 2.0 copy-start.1
Sparse Core Ops, SparseCore 0:
  9.6 20.8 all-gather.4
  32.1 25.5 all-gather.2
where the time goes:
time: 268 us; the launch traced here: 266 us
  blocking collectives  68.8 us (26%)
  matrix products  64.2 us (24%)
  local copies, waits for them, and re-layouts  45.8 us (17%)
  loops' own time  36.8 us (14%)
  other arithmetic  17.3 us (6%)
  between operations  14.3 us (5%)
  starting transfers between devices  11 us (4%)
  waiting for transfers between devices  8.01 us (3%)
    another operation x2, loops' own time, attend(): lax.map(single_head, (query_heads, jnp.arange(head_count, dtype=jnp.int32)))  36.8 us
    dot_general x20, matrix products, single_head(): jnp.dot(query_head, key_head.T, preferred_element_type=jnp.float32)  30.5 us
    dot_general x6, matrix products, project(): product = jnp.dot(hidden, weight, preferred_element_type=jnp.float32)  25.9 us
    all_gather x1, blocking collectives, local(): lax.all_gather(key_comp, 'seq', axis=0, tiled=True)  22.7 us
    all_gather x1, blocking collectives, local(): lax.all_gather(key_prompt, 'seq', axis=0, tiled=True)  16.2 us
    all_gather x1, blocking collectives, local(): lax.all_gather(value_comp, 'seq', axis=0, tiled=True)  15.1 us
    dynamic_update_slice x40, local copies, waits for them, and re-layouts, attend(): lax.map(single_head, (query_heads, jnp.arange(head_count, dtype=jnp.int32)))  14.9 us
    all_gather x1, blocking collectives, local(): lax.all_gather(value_prompt, 'seq', axis=0, tiled=True)  14.8 us
  transfers between devices with their start and end apart: 4, of which 2 were waited for; matrix products, arithmetic and copies ran while one was open for 11% of the time, Pallas kernels for 0%

commit v1 on v0

v1 whole, which is shorter than its diff:
```python
import functools
import math

import jax
import jax.numpy as jnp
import numpy as np
from jax import lax
from jax.experimental import pallas as pl
from jax.experimental.pallas import tpu as pltpu
from jax.sharding import PartitionSpec as P

HD = 128
HALF = HD // 2
LONGEST = 256
ROPE_BASE = 1000000.0
MESH = pl.DeviceIdType.MESH
BF16 = jnp.bfloat16
F32 = jnp.float32
NEG = -1e30


def dot(a, b):
    return jnp.dot(a, b, preferred_element_type=F32)


def dot_t(a, b):
    return lax.dot_general(a, b, (((1,), (1,)), ((), ())), preferred_element_type=F32)


def kernel(
    cfg,
    hp_ref, hc_ref, wq_ref, wk_ref, wv_ref, len_ref, own_ref, freq_ref,
    po_ref, co_ref,
    hid, wq, wk, wv, cosb, sinb, qb, kv, ckv, scat, sendb,
    w_sem, own_sem, x_send, x_recv, f_send, zr_send, zr_recv, zl_send, zl_recv,
    c_send, c_recv, a_send, a_recv,
):
    n_mp, n_seq, prows, crows, feat, qcols, kcols, ncomp = cfg
    nheads, nkv = qcols // HD, kcols // HD
    group = nheads // nkv
    cap = 2 * crows // n_seq
    chunk = crows
    npc = prows // chunk
    nchunk = npc + 1
    back = min(-(-(LONGEST - 1) // crows), n_seq - 1)
    s = lax.axis_index("seq")
    m = lax.axis_index("mp")
    core = lax.rem(m, 2)
    sib = m + 1 - 2 * core
    nx = n_mp // 2

    def peer(k):
        return lax.rem(m + 2 * k, n_mp)

    def seq_at(k):
        return lax.rem(s + k + n_seq, n_seq)

    barrier = pltpu.get_barrier_semaphore()
    pl.semaphore_signal(barrier, inc=1, device_id={"mp": sib}, device_id_type=MESH)
    for k in range(1, nx):
        pl.semaphore_signal(barrier, inc=1, device_id={"mp": peer(k)}, device_id_type=MESH)
    for k in range(1, n_seq):
        pl.semaphore_signal(barrier, inc=1, device_id={"seq": seq_at(k)}, device_id_type=MESH)

    def rows_of(c):
        return pl.ds(c * chunk, chunk)

    def source(c):
        return hp_ref.at[rows_of(c)] if c < npc else hc_ref

    own_copies = [
        pltpu.make_async_copy(source(c), hid.at[m, rows_of(c)], own_sem.at[c]) for c in range(nchunk)
    ]
    for copy in own_copies:
        copy.start()
    w_copies = [
        pltpu.make_async_copy(wk_ref, wk, w_sem.at[0]),
        pltpu.make_async_copy(wv_ref, wv, w_sem.at[1]),
        pltpu.make_async_copy(wq_ref, wq, w_sem.at[2]),
    ]

    pl.semaphore_wait(barrier, n_seq + nx - 1)

    def x_copy(c, k):
        target = sib if k == 0 else peer(k)
        return pltpu.make_async_remote_copy(
            src_ref=source(c), dst_ref=hid.at[m, rows_of(c)],
            send_sem=x_send.at[c, k], recv_sem=x_recv.at[c, k],
            device_id={"mp": target}, device_id_type=MESH,
        )

    def f_copy(c, k):
        held = lax.rem(m - 2 * k + 2 * n_mp, n_mp)
        return pltpu.make_async_remote_copy(
            src_ref=hid.at[held, rows_of(c)], dst_ref=hid.at[held, rows_of(c)],
            send_sem=f_send.at[c, k - 1], recv_sem=x_recv.at[c, nx - 1 + k],
            device_id={"mp": sib}, device_id_type=MESH,
        )

    for c in range(nchunk):
        for k in list(range(1, nx)) + [0]:
            x_copy(c, k).start()
    for copy in w_copies:
        copy.start()

    ii = lax.broadcasted_iota(jnp.int32, (ncomp, ncomp), 0)
    jj = lax.broadcasted_iota(jnp.int32, (ncomp, ncomp), 1)
    lens = jnp.broadcast_to(len_ref[...], (ncomp, ncomp))
    ends_col = jnp.sum(jnp.where(jj <= ii, lens, 0), 1, keepdims=True)
    ends_row = jnp.sum(jnp.where(ii == jj, jnp.broadcast_to(ends_col, (ncomp, ncomp)), 0), 0, keepdims=True)
    crow = s * crows + lax.broadcasted_iota(jnp.int32, (crows, 1), 0)
    ends_all = jnp.broadcast_to(ends_row, (crows, ncomp))
    starts = jnp.max(jnp.where(ends_all <= crow, ends_all, 0), 1, keepdims=True)
    freq = freq_ref[...]
    sign = jnp.where(lax.broadcasted_iota(jnp.int32, (1, HD), 1) < HALF, -1.0, 1.0)
    for c in range(nchunk):
        if c < npc:
            pos = s * prows + c * chunk + lax.broadcasted_iota(jnp.int32, (chunk, 1), 0)
        else:
            pos = n_seq * prows + crow - starts
        angle = pos.astype(F32) * freq
        cosb[rows_of(c)] = jnp.cos(angle)
        sinb[rows_of(c)] = jnp.sin(angle) * sign

    ri = lax.broadcasted_iota(jnp.int32, (crows, crows), 0)
    rj = lax.broadcasted_iota(jnp.int32, (crows, crows), 1)
    own_i = jnp.broadcast_to(own_ref[...], (crows, crows))
    own_row = jnp.sum(jnp.where(ri == rj, own_i, 0), 0, keepdims=True)
    earlier = jnp.where((own_i == own_row) & (ri < rj), 1, 0)
    slot_row = own_row * cap + jnp.sum(earlier, 0, keepdims=True)
    slots = lax.broadcasted_iota(jnp.int32, (n_seq * cap, crows), 0)
    scat[...] = jnp.where(slots == slot_row, 1.0, 0.0).astype(BF16)

    def zr_copy(c, d):
        t = lax.rem(s - d + 1 + n_seq, n_seq)
        return pltpu.make_async_remote_copy(
            src_ref=kv.at[t, rows_of(c)], dst_ref=kv.at[t, rows_of(c)],
            send_sem=zr_send.at[c, d - 1], recv_sem=zr_recv.at[c, d - 1],
            device_id={"seq": seq_at(1)}, device_id_type=MESH,
        )

    def zl_copy(c, d):
        t = lax.rem(s + d - 1, n_seq)
        return pltpu.make_async_remote_copy(
            src_ref=kv.at[t, rows_of(c)], dst_ref=kv.at[t, rows_of(c)],
            send_sem=zl_send.at[c, d - 1], recv_sem=zl_recv.at[c, d - 1],
            device_id={"seq": seq_at(-1)}, device_id_type=MESH,
        )

    def zr_in(c, d):
        t = lax.rem(s - d + n_seq, n_seq)
        return pltpu.make_async_remote_copy(
            src_ref=kv.at[t, rows_of(c)], dst_ref=kv.at[t, rows_of(c)],
            send_sem=zr_send.at[c, d - 1], recv_sem=zr_recv.at[c, d - 1],
            device_id={"seq": seq_at(1)}, device_id_type=MESH,
        )

    def zl_in(c, d):
        t = lax.rem(s + d, n_seq)
        return pltpu.make_async_remote_copy(
            src_ref=kv.at[t, rows_of(c)], dst_ref=kv.at[t, rows_of(c)],
            send_sem=zl_send.at[c, d - 1], recv_sem=zl_recv.at[c, d - 1],
            device_id={"seq": seq_at(-1)}, device_id_type=MESH,
        )

    def z_first(c):
        @pl.when(s < n_seq - 1)
        def _():
            zr_copy(c, 1).start()

        @pl.when(s > 0)
        def _():
            zl_copy(c, 1).start()

    def z_step(c, d):
        @pl.when(s >= d)
        def _():
            zr_in(c, d).wait_recv()

            if d < n_seq - 1:
                @pl.when(s < n_seq - 1)
                def _():
                    zr_copy(c, d + 1).start()

        @pl.when(s + d < n_seq)
        def _():
            zl_in(c, d).wait_recv()

            if d < n_seq - 1:
                @pl.when(s > 0)
                def _():
                    zl_copy(c, d + 1).start()

    def c_copy(d):
        return pltpu.make_async_remote_copy(
            src_ref=ckv.at[back], dst_ref=ckv.at[back - d],
            send_sem=c_send.at[d - 1], recv_sem=c_recv.at[d - 1],
            device_id={"seq": seq_at(d)}, device_id_type=MESH,
        )

    for d in range(1, back + 1):
        @pl.when(s < d)
        def _():
            ckv[back - d] = jnp.zeros((crows, 2 * kcols), BF16)

    def product(c, weight, cols):
        total = None
        for q in range(n_mp):
            part = dot(hid[q, c * chunk:(c + 1) * chunk, :], weight[q * feat:(q + 1) * feat, cols])
            total = part if total is None else total + part
        return total

    def rope(x, c):
        cos = cosb[c * chunk:(c + 1) * chunk, :]
        sin = sinb[c * chunk:(c + 1) * chunk, :]
        return (x * cos + pltpu.roll(x, HALF, 1) * sin).astype(BF16)

    kw = kcols
    qw = 2 * HD if nheads % 2 == 0 else HD

    for c in range(nchunk):
        own_copies[c].wait()
        for k in range(1, nx):
            x_copy(c, k).wait_recv()
            f_copy(c, k).start()
        x_copy(c, 0).wait_recv()
        for k in range(1, nx):
            f_copy(c, k).wait_recv()
        if c == 0:
            w_copies[0].wait()
            w_copies[1].wait()
        kp = product(c, wk, slice(None))
        keys = [rope(kp[:, h * HD:(h + 1) * HD], c) for h in range(nkv)]
        vals = product(c, wv, slice(None)).astype(BF16)
        if c < npc:
            for h in range(nkv):
                kv[s, c * chunk:(c + 1) * chunk, h * HD:(h + 1) * HD] = keys[h]
            kv[s, c * chunk:(c + 1) * chunk, kcols:] = vals
            z_first(c)
        else:
            for h in range(nkv):
                ckv[back, :, h * HD:(h + 1) * HD] = keys[h]
            ckv[back, :, kcols:] = vals
            for d in range(1, back + 1):
                @pl.when(s + d < n_seq)
                def _():
                    c_copy(d).start()
        if c == 0:
            w_copies[2].wait()

        def q_tile(t, carry):
            qp = product(c, wq, pl.ds(pl.multiple_of(t * qw, qw), qw))
            for h in range(qw // HD):
                qb[t * (qw // HD) + h, c * chunk:(c + 1) * chunk, :] = rope(qp[:, h * HD:(h + 1) * HD], c)
            return carry

        lax.fori_loop(0, qcols // qw, q_tile, 0)
        if c < npc:
            z_step(c, 1)
        if c >= 1:
            for d in range(2, n_seq):
                z_step(c - 1, d)

    scale = HD ** -0.5 * math.log2(math.e)
    total_keys = n_seq * prows

    for d in range(1, back + 1):
        @pl.when(s >= d)
        def _():
            c_copy(d).wait_recv()

    nck = (back + 1) * crows
    ckey = (s - back) * crows + lax.broadcasted_iota(jnp.int32, (crows, nck), 1)
    cmask = jnp.where((ckey >= starts) & (ckey <= crow), 0.0, NEG)

    def a_copy(g, k):
        o = seq_at(k)
        return pltpu.make_async_remote_copy(
            src_ref=sendb.at[g, pl.ds(pl.multiple_of(o * cap, cap), cap)],
            dst_ref=co_ref.at[pl.ds(pl.multiple_of(s * cap, cap), cap), pl.ds(g * group * HD, group * HD)],
            send_sem=a_send.at[g, k - 1], recv_sem=a_recv.at[g, k - 1],
            device_id={"seq": o}, device_id_type=MESH,
        )

    def a_in(g, k):
        o = seq_at(-k)
        return pltpu.make_async_remote_copy(
            src_ref=sendb.at[g, pl.ds(pl.multiple_of(o * cap, cap), cap)],
            dst_ref=co_ref.at[pl.ds(pl.multiple_of(o * cap, cap), cap), pl.ds(g * group * HD, group * HD)],
            send_sem=a_send.at[g, k - 1], recv_sem=a_recv.at[g, k - 1],
            device_id={"seq": o}, device_id_type=MESH,
        )

    for g in range(nkv):
        kcol = slice(g * HD, (g + 1) * HD)
        vcol = slice(kcols + g * HD, kcols + (g + 1) * HD)
        for h in range(group):
            q = qb[g * group + h, npc * chunk:(npc + 1) * chunk, :]
            sp = dot_t(q, kv[:, :, kcol].reshape(total_keys, HD)) * scale
            sc = dot_t(q, ckv[:, :, kcol].reshape(nck, HD)) * scale + cmask
            top = jnp.maximum(jnp.max(sp, 1, keepdims=True), jnp.max(sc, 1, keepdims=True))
            ep = jnp.exp2(sp - top)
            ec = jnp.exp2(sc - top)
            total = jnp.sum(ep, 1, keepdims=True) + jnp.sum(ec, 1, keepdims=True)
            mixed = dot(ep.astype(BF16), kv[:, :, vcol].reshape(total_keys, HD))
            mixed = mixed + dot(ec.astype(BF16), ckv[:, :, vcol].reshape(nck, HD))
            out = (mixed / total).astype(BF16)
            sendb[g, :, h * HD:(h + 1) * HD] = dot(scat[...], out).astype(BF16)
        for k in range(1, n_seq):
            a_copy(g, k).start()
        mine = pl.ds(pl.multiple_of(s * cap, cap), cap)
        co_ref[mine, g * group * HD:(g + 1) * group * HD] = sendb[g, mine, :]

    ppos = s * prows + lax.broadcasted_iota(jnp.int32, (prows, 1), 0)
    pkey = lax.broadcasted_iota(jnp.int32, (prows, total_keys), 1)
    for g in range(nkv):
        kcol = slice(g * HD, (g + 1) * HD)
        vcol = slice(kcols + g * HD, kcols + (g + 1) * HD)
        for h in range(group):
            head = g * group + h
            q = qb[head, :prows, :]
            sp = dot_t(q, kv[:, :, kcol].reshape(total_keys, HD)) * scale
            sp = jnp.where(pkey <= ppos, sp, NEG)
            top = jnp.max(sp, 1, keepdims=True)
            ep = jnp.exp2(sp - top)
            total = jnp.sum(ep, 1, keepdims=True)
            mixed = dot(ep.astype(BF16), kv[:, :, vcol].reshape(total_keys, HD))
            po_ref[:, head * HD:(head + 1) * HD] = (mixed / total).astype(BF16)

    for g in range(nkv):
        for k in range(1, n_seq):
            a_in(g, k).wait_recv()
    for g in range(nkv):
        for k in range(1, n_seq):
            a_copy(g, k).wait_send()
    for c in range(nchunk):
        for k in range(nx):
            x_copy(c, k).wait_send()
        for k in range(1, nx):
            f_copy(c, k).wait_send()
    for c in range(npc):
        for d in range(1, n_seq):
            @pl.when((s - d + 1 >= 0) & (s < n_seq - 1))
            def _():
                zr_copy(c, d).wait_send()

            @pl.when((s + d - 1 < n_seq) & (s > 0))
            def _():
                zl_copy(c, d).wait_send()
    for d in range(1, back + 1):
        @pl.when(s + d < n_seq)
        def _():
            c_copy(d).wait_send()


def local(n_mp, n_seq, hidden_prompt, hidden_comp, w_query, w_key, w_value, lengths, row_owner):
    prows, feat = hidden_prompt.shape
    crows = hidden_comp.shape[0]
    depth, qcols = w_query.shape
    kcols = w_key.shape[1]
    ncomp = lengths.shape[0]
    nkv = kcols // HD
    group = qcols // kcols
    cap = 2 * crows // n_seq
    npc = prows // crows
    nchunk = npc + 1
    nx = n_mp // 2
    back = min(-(-(LONGEST - 1) // crows), n_seq - 1)
    half = ROPE_BASE ** (-2.0 * np.arange(HALF, dtype=np.float64) / HD)
    freq = jnp.asarray(np.concatenate([half, half])[None, :], F32)
    cfg = (n_mp, n_seq, prows, crows, feat, qcols, kcols, ncomp)
    hbm = pl.BlockSpec(memory_space=pl.ANY)
    vmem = pl.BlockSpec(memory_space=pltpu.VMEM)
    dma = lambda *shape: pltpu.SemaphoreType.DMA(shape)
    rows = prows + crows
    z_hops = max(n_seq - 1, 1)
    return pl.pallas_call(
        functools.partial(kernel, cfg),
        out_shape=(
            jax.ShapeDtypeStruct((prows, qcols), BF16),
            jax.ShapeDtypeStruct((n_seq * cap, qcols), BF16),
        ),
        in_specs=[hbm] * 5 + [vmem] * 3,
        out_specs=(vmem, vmem),
        scratch_shapes=[
            pltpu.VMEM((n_mp, rows, feat), BF16),
            pltpu.VMEM((depth, qcols), BF16),
            pltpu.VMEM((depth, kcols), BF16),
            pltpu.VMEM((depth, kcols), BF16),
            pltpu.VMEM((rows, HD), F32),
            pltpu.VMEM((rows, HD), F32),
            pltpu.VMEM((qcols // HD, rows, HD), BF16),
            pltpu.VMEM((n_seq, prows, 2 * kcols), BF16),
            pltpu.VMEM((back + 1, crows, 2 * kcols), BF16),
            pltpu.VMEM((n_seq * cap, crows), BF16),
            pltpu.VMEM((nkv, n_seq * cap, group * HD), BF16),
            dma(3),
            dma(nchunk),
            dma(nchunk, nx),
            dma(nchunk, 2 * nx - 1),
            dma(nchunk, nx - 1),
            dma(npc, z_hops), dma(npc, z_hops), dma(npc, z_hops), dma(npc, z_hops),
            dma(back), dma(back),
            dma(nkv, z_hops), dma(nkv, z_hops),
        ],
        compiler_params=pltpu.CompilerParams(
            collective_id=0, has_side_effects=True, vmem_limit_bytes=56 * 1024 * 1024
        ),
        cost_estimate=pl.CostEstimate(
            flops=2 * rows * depth * (qcols + 2 * kcols), bytes_accessed=2 * depth * (qcols + 2 * kcols), transcendentals=0
        ),
        name="grouped_attention",
    )(hidden_prompt, hidden_comp, w_query, w_key, w_value, lengths.reshape(1, ncomp), row_owner, freq)


def solution(mesh):
    placed = (
        P(("groups", "seq"), "mp"),
        P(("groups", "seq"), "mp"),
        P(None, "mp"),
        P(None, "mp"),
        P(None, "mp"),
        P("groups"),
        P(("groups", "seq"), None),
    )
    return jax.shard_map(
        functools.partial(local, mesh.shape["mp"], mesh.shape["seq"]),
        mesh=mesh,
        in_specs=placed,
        out_specs=(P(("groups", "seq"), "mp"), P(("groups", "seq"), "mp")),
        check_vma=False,
    )
```

time: 268 us -> 72.8 us (0.27)
  blocking collectives: 68.8 us -> 0 us
  Pallas kernels: 0 us -> 66.6 us
  matrix products: 64.2 us -> 0 us
  local copies, waits for them, and re-layouts: 45.8 us -> 5.32 us
  loops' own time: 36.8 us -> 0 us
  other arithmetic: 17.3 us -> 0 us
  between operations: 14.3 us -> 0.64 us
  starting transfers between devices: 11 us -> 0 us
  waiting for transfers between devices: 8.01 us -> 0 us
    all_gather x4 -> x0, blocking collectives: 68.8 us -> none  [the longest x1 22.7 us: local(): lax.all_gather(key_comp, 'seq', axis=0, tiled=True)]
    pallas_call x0 -> x1, Pallas kernels: none -> 66.6 us  [local(): pl.pallas_call(functools.partial(kernel, cfg), out_shape=(jax.ShapeDtypeS...]
    dot_general x46 -> x0, matrix products: 64.2 us -> none  [the longest x20 30.5 us: single_head(): jnp.dot(query_head, key_head.T, preferred_element_type=jnp.float32)]
    another operation x2 -> x0, loops' own time: 36.8 us -> none  [attend(): lax.map(single_head, (query_heads, jnp.arange(head_count, dtype=jnp.int32)))]
    dynamic_update_slice x40 -> x0, local copies, waits for them, and re-layouts: 14.9 us -> none  [attend(): lax.map(single_head, (query_heads, jnp.arange(head_count, dtype=jnp.int32)))]
    dynamic_slice x20 -> x0, local copies, waits for them, and re-layouts: 11.7 us -> none  [attend(): lax.map(single_head, (query_heads, jnp.arange(head_count, dtype=jnp.int32)))]
    all_to_all x2 -> x0, starting transfers between devices: 10.9 us -> none  [the longest x1 6.32 us: local(): lax.all_to_all(rows_sent, 'seq', split_axis=0, concat_axis=0, tiled=True)]
    reduce_sum x23 -> x0, other arithmetic: 8.4 us -> none  [the longest x20 6.74 us: single_head(): row_total = jnp.sum(weights, 1, keepdims=True)]
  transfers between devices with their start and end apart: 4 -> 0, of which waited for: 2 -> 0; matrix products, arithmetic and copies ran while one was open for 11% -> 0% of each run, Pallas kernels for 0% -> 0%
where the time goes in v1:
time: 72.8 us; the launch traced here: 72.6 us
  Pallas kernels  66.6 us (91%)
  local copies, waits for them, and re-layouts  5.32 us (7%)
    pallas_call x1, Pallas kernels, local(): pl.pallas_call(functools.partial(kernel, cfg), out_shape=(jax.ShapeDtypeS...  66.6 us
    unnamed x3, local copies, waits for them, and re-layouts  5.32 us

profile of v1, /device:TPU:0, one launch (start us, length us, event | category | flops | bytes accessed | tf_op | source)
XLA Modules:
  0.0 72.6 jit_solution(6969757193587978615)
XLA Ops:
  0.6 1.4 %copy.10.own_ref = s32[128,1]{1,0:T(8,128)} copy(s32[128,1]{0,1:T(1,128)} %param.14) | data formatting | bytes 1024 | tf_op args[6]
  2.0 66.6 %grouped_attention.1 = (bf16[256,1280]{1,0:T(8,128)(2,1)}, bf16[256,1280]{1,0:T(8,128)(2,1)}) custom-call(bf16[256,1280]{1,0:T(8,128)(2,1)} %hp_ref.1, bf16[128,1280]{1,0:T(8,128)(2,1)} %hc_ref.1, bf16[5120,1280]{1,0:T(8,128)(2,1)} %wq_ref.1, bf16[5120,256]{1,0:T(8,128)(2,1)} %wk_ref.1, bf16[5120,256]{1,0:T(8,128)(2,1)} %wv_ref.1, s32[1,16]{1,0:T(1,128)} %bitcast.1, ...), custom_call_target="tpu_custom_call" | custom-call | flops 7046430720 | bytes 18350080 | tf_op jit(solution)/shard_map/grouped_attention/pallas_call | solution.py:377
  68.6 2.0 %copy.13 = bf16[256,1280]{1,0:T(8,128)(2,1)} copy(bf16[256,1280]{1,0:T(8,128)(2,1)} %get-tuple-element.4) | data formatting | bytes 1310720
  70.6 2.0 %copy.14 = bf16[256,1280]{1,0:T(8,128)(2,1)} copy(bf16[256,1280]{1,0:T(8,128)(2,1)} %get-tuple-element.5) | data formatting | bytes 1310720

commit v2 on v1

--- a/solution.py
+++ b/solution.py
@@ -17,6 +17,7 @@
 BF16 = jnp.bfloat16
 F32 = jnp.float32
 NEG = -1e30
+PIECES = 4
 
 
 def dot(a, b):
@@ -31,7 +32,7 @@
     cfg,
     hp_ref, hc_ref, wq_ref, wk_ref, wv_ref, len_ref, own_ref, freq_ref,
     po_ref, co_ref,
-    hid, wq, wk, wv, cosb, sinb, qb, kv, ckv, scat, sendb,
+    hid, wq, wk, wv, cosb, sinb, qb, kv, ckv, scat, sendb, tops, sums, mixes,
     w_sem, own_sem, x_send, x_recv, f_send, zr_send, zr_recv, zl_send, zl_recv,
     c_send, c_recv, a_send, a_recv,
 ):
@@ -124,9 +125,10 @@
 
     ri = lax.broadcasted_iota(jnp.int32, (crows, crows), 0)
     rj = lax.broadcasted_iota(jnp.int32, (crows, crows), 1)
-    own_i = jnp.broadcast_to(own_ref[...], (crows, crows))
-    own_row = jnp.sum(jnp.where(ri == rj, own_i, 0), 0, keepdims=True)
-    earlier = jnp.where((own_i == own_row) & (ri < rj), 1, 0)
+    own_row = own_ref[...]
+    own_all = jnp.broadcast_to(own_row, (crows, crows))
+    own_col = jnp.sum(jnp.where(ri == rj, own_all, 0), 1, keepdims=True)
+    earlier = jnp.where((own_col == own_all) & (ri < rj), 1, 0)
     slot_row = own_row * cap + jnp.sum(earlier, 0, keepdims=True)
     slots = lax.broadcasted_iota(jnp.int32, (n_seq * cap, crows), 0)
     scat[...] = jnp.where(slots == slot_row, 1.0, 0.0).astype(BF16)
@@ -254,16 +256,41 @@
                 qb[t * (qw // HD) + h, c * chunk:(c + 1) * chunk, :] = rope(qp[:, h * HD:(h + 1) * HD], c)
             return carry
 
-        lax.fori_loop(0, qcols // qw, q_tile, 0)
+        tiles = qcols // qw
+        lax.fori_loop(0, tiles // 2, q_tile, 0)
+        if c >= 1 and n_seq > 2:
+            z_step(c - 1, 2)
+        lax.fori_loop(tiles // 2, tiles, q_tile, 0)
         if c < npc:
             z_step(c, 1)
-        if c >= 1:
-            for d in range(2, n_seq):
-                z_step(c - 1, d)
 
     scale = HD ** -0.5 * math.log2(math.e)
     total_keys = n_seq * prows
-
+    early = (npc - 1) * chunk
+
+    for c in range(npc - 1):
+        for d in range(3, n_seq):
+            z_step(c, d)
+
+    def key_block(g, first, stop):
+        return kv[:, first:stop, g * HD:(g + 1) * HD].reshape(n_seq * (stop - first), HD)
+
+    def value_block(g, first, stop):
+        return kv[:, first:stop, kcols + g * HD:kcols + (g + 1) * HD].reshape(n_seq * (stop - first), HD)
+
+    for g in range(nkv):
+        for h in range(group):
+            head = g * group + h
+            q = qb[head, npc * chunk:(npc + 1) * chunk, :]
+            sp = dot_t(q, key_block(g, 0, early)) * scale
+            top = jnp.max(sp, 1, keepdims=True)
+            ep = jnp.exp2(sp - top)
+            tops[head] = jnp.broadcast_to(top, (crows, HD))
+            sums[head] = jnp.broadcast_to(jnp.sum(ep, 1, keepdims=True), (crows, HD))
+            mixes[head] = dot(ep.astype(BF16), value_block(g, 0, early))
+
+    for d in range(3, n_seq):
+        z_step(npc - 1, d)
     for d in range(1, back + 1):
         @pl.when(s >= d)
         def _():
@@ -295,15 +322,19 @@
         kcol = slice(g * HD, (g + 1) * HD)
         vcol = slice(kcols + g * HD, kcols + (g + 1) * HD)
         for h in range(group):
-            q = qb[g * group + h, npc * chunk:(npc + 1) * chunk, :]
-            sp = dot_t(q, kv[:, :, kcol].reshape(total_keys, HD)) * scale
+            head = g * group + h
+            q = qb[head, npc * chunk:(npc + 1) * chunk, :]
+            sp = dot_t(q, key_block(g, early, prows)) * scale
             sc = dot_t(q, ckv[:, :, kcol].reshape(nck, HD)) * scale + cmask
+            before = tops[head][:, :1]
             top = jnp.maximum(jnp.max(sp, 1, keepdims=True), jnp.max(sc, 1, keepdims=True))
+            top = jnp.maximum(top, before)
             ep = jnp.exp2(sp - top)
             ec = jnp.exp2(sc - top)
-            total = jnp.sum(ep, 1, keepdims=True) + jnp.sum(ec, 1, keepdims=True)
-            mixed = dot(ep.astype(BF16), kv[:, :, vcol].reshape(total_keys, HD))
-            mixed = mixed + dot(ec.astype(BF16), ckv[:, :, vcol].reshape(nck, HD))
+            shrink = jnp.exp2(before - top)
+            total = jnp.sum(ep, 1, keepdims=True) + jnp.sum(ec, 1, keepdims=True) + sums[head][:, :1] * shrink
+            mixed = dot(ep.astype(BF16), value_block(g, early, prows))
+            mixed = mixed + dot(ec.astype(BF16), ckv[:, :, vcol].reshape(nck, HD)) + mixes[head] * shrink
             out = (mixed / total).astype(BF16)
             sendb[g, :, h * HD:(h + 1) * HD] = dot(scat[...], out).astype(BF16)
         for k in range(1, n_seq):
@@ -351,6 +382,25 @@
         @pl.when(s + d < n_seq)
         def _():
             c_copy(d).wait_send()
+
+
+def hand_over(po_in, co_in, po_ref, co_ref, stage, in_sem, out_sem):
+    pieces = in_sem.shape[1]
+    reads, writes = [], []
+    for i, (src, dst) in enumerate(((po_in, po_ref), (co_in, co_ref))):
+        step = src.shape[0] // pieces
+        for p in range(pieces):
+            part = pl.ds(p * step, step)
+            held = stage.at[i, part]
+            reads.append(pltpu.make_async_copy(src.at[part], held, in_sem.at[i, p]))
+            writes.append(pltpu.make_async_copy(held, dst.at[part], out_sem.at[i, p]))
+    for read in reads:
+        read.start()
+    for read, write in zip(reads, writes):
+        read.wait()
+        write.start()
+    for write in writes:
+        write.wait()
 
 
 def local(n_mp, n_seq, hidden_prompt, hidden_comp, w_query, w_key, w_value, lengths, row_owner):
@@ -374,7 +424,7 @@
     dma = lambda *shape: pltpu.SemaphoreType.DMA(shape)
     rows = prows + crows
     z_hops = max(n_seq - 1, 1)
-    return pl.pallas_call(
+    results = pl.pallas_call(
         functools.partial(kernel, cfg),
         out_shape=(
             jax.ShapeDtypeStruct((prows, qcols), BF16),
@@ -394,6 +444,9 @@
             pltpu.VMEM((back + 1, crows, 2 * kcols), BF16),
             pltpu.VMEM((n_seq * cap, crows), BF16),
             pltpu.VMEM((nkv, n_seq * cap, group * HD), BF16),
+            pltpu.VMEM((qcols // HD, crows, HD), F32),
+            pltpu.VMEM((qcols // HD, crows, HD), F32),
+            pltpu.VMEM((qcols // HD, crows, HD), F32),
             dma(3),
             dma(nchunk),
             dma(nchunk, nx),
@@ -410,7 +463,15 @@
             flops=2 * rows * depth * (qcols + 2 * kcols), bytes_accessed=2 * depth * (qcols + 2 * kcols), transcendentals=0
         ),
         name="grouped_attention",
-    )(hidden_prompt, hidden_comp, w_query, w_key, w_value, lengths.reshape(1, ncomp), row_owner, freq)
+    )(hidden_prompt, hidden_comp, w_query, w_key, w_value, lengths.reshape(1, ncomp), row_owner.reshape(1, crows), freq)
+    return pl.pallas_call(
+        hand_over,
+        out_shape=tuple(jax.ShapeDtypeStruct(r.shape, BF16) for r in results),
+        in_specs=[hbm] * 2,
+        out_specs=(hbm, hbm),
+        scratch_shapes=[pltpu.VMEM((2, max(prows, n_seq * cap), qcols), BF16), dma(2, PIECES), dma(2, PIECES)],
+        name="hand_over",
+    )(*results)
 
 
 def solution(mesh):

time: 72.8 us -> 62.7 us (0.86)
  local copies, waits for them, and re-layouts: 5.32 us -> 0 us
  Pallas kernels: 66.6 us -> 61.7 us
    pallas_call x1, Pallas kernels: 66.6 us -> 59.5 us  [local(): pl.pallas_call(functools.partial(kernel, cfg), out_shape=(jax.ShapeDtypeS...]
    unnamed x3 -> x0, local copies, waits for them, and re-layouts: 5.32 us -> none
    pallas_call x0 -> x1, Pallas kernels: none -> 2.2 us  [local(): pl.pallas_call(hand_over, out_shape=tuple((jax.ShapeDtypeStruct(r.shape,...]
where the time goes in v2:
time: 62.7 us; the launch traced here: 62.5 us
  Pallas kernels  61.7 us (98%)
  between operations  0.8 us (1%)
    pallas_call x1, Pallas kernels, local(): pl.pallas_call(functools.partial(kernel, cfg), out_shape=(jax.ShapeDtypeS...  59.5 us
    pallas_call x1, Pallas kernels, local(): pl.pallas_call(hand_over, out_shape=tuple((jax.ShapeDtypeStruct(r.shape,...  2.2 us

profile of v2, /device:TPU:0, one launch (start us, length us, event | category | flops | bytes accessed | tf_op | source)
XLA Modules:
  0.0 62.5 jit_solution(7812382583239760980)
XLA Ops:
  0.6 59.5 %grouped_attention.1 = (bf16[256,1280]{1,0:T(8,128)(2,1)}, bf16[256,1280]{1,0:T(8,128)(2,1)}) custom-call(bf16[256,1280]{1,0:T(8,128)(2,1)} %hp_ref.1, bf16[128,1280]{1,0:T(8,128)(2,1)} %hc_ref.1, bf16[5120,1280]{1,0:T(8,128)(2,1)} %wq_ref.1, bf16[5120,256]{1,0:T(8,128)(2,1)} %wk_ref.1, bf16[5120,256]{1,0:T(8,128)(2,1)} %wv_ref.1, s32[1,16]{1,0:T(1,128)} %bitcast.2, ...), custom_call_target="tpu_custom_call" | custom-call | flops 7046430720 | bytes 18350080 | tf_op jit(solution)/shard_map/grouped_attention/pallas_call | solution.py:427
  60.1 2.2 %hand_over.1 = (bf16[256,1280]{1,0:T(8,128)(2,1)}, bf16[256,1280]{1,0:T(8,128)(2,1)}) custom-call(bf16[256,1280]{1,0:T(8,128)(2,1)} %get-tuple-element.4.po_in, bf16[256,1280]{1,0:T(8,128)(2,1)} %get-tuple-element.5.co_in), custom_call_target="tpu_custom_call" | custom-call | tf_op jit(solution)/shard_map/hand_over/pallas_call | solution.py:467
